TPU v7x, 256 devices: a whole 4x4x8 slice. The times are simulated.
256 devices in a mesh: seq: 64 (over x, y, z_hi, core), ch: 4 (over z_lo).
Axes of the slice: x: 4, y: 4, z: 8 (z_hi: 2, z_lo: 4; z = z_hi * 4 + z_lo), core: 2. Of those that a mesh axis runs over, the one named last changes fastest.
Arguments:
- values: bfloat16 [16384, 2048], P('seq', 'ch'), may hold values from -7.5 to 7.5
- gates: bfloat16 [16384, 2048], P('seq', 'ch'), may hold values from -6 to 6
- filters: float32 [16384, 2048], P('seq', 'ch'), may hold values from -1.1 to 1.1
- skip: float32 [2048], P('ch'), may hold values from -4 to 4
- cotangent: bfloat16 [16384, 2048], P('seq', 'ch'), may hold values from -6 to 6
- flagged: int32 [16384], P('seq'), may hold values 0 or 1
Outputs:
- mixed: bfloat16 [16384, 2048], P('seq', 'ch')
- value_grad: bfloat16 [16384, 2048], P('seq', 'ch')
- gate_grad: bfloat16 [16384, 2048], P('seq', 'ch')
- filter_grad: float32 [16384, 2048], P('seq', 'ch')
- skip_grad: float32 [2048], P('ch')
All inputs are finite; a program needn't handle non-finite values. No bound on the sum of `flagged` on one device may be relied on, other than what follows from the above.
Results may differ from a plain program's by a relative error of at most 0.001.
Values sent between devices are 32-bit elements; how exact they have to be, the bound alone decides.
A program may use at most 128 MiB of HBM per device.

v0:
```python
import math

import jax
import jax.numpy as jnp
from jax import lax
from jax.sharding import PartitionSpec as P


def partner(array, axis, apart):
    return lax.ppermute(array, axis, [(i, i ^ 1 << apart) for i in range(lax.axis_size(axis))])


def matmul(form, left, right):
    return jnp.einsum(form, left, right, precision=lax.Precision.HIGHEST)


def dft_table(out_count, in_count, modulus, sign):
    outer = jnp.arange(out_count, dtype=jnp.int32)[:, None]
    inner = jnp.arange(in_count, dtype=jnp.int32)[None, :]
    angles = (outer * inner % modulus).astype(jnp.float32) * (2.0 * math.pi / modulus)
    return (jnp.cos(angles), sign * jnp.sin(angles))


def rotate(real_part, imag_part, angles, sign):
    cosine = jnp.cos(angles)
    sine = sign * jnp.sin(angles)
    return (real_part * cosine - imag_part * sine, real_part * sine + imag_part * cosine)


def flip_blocks(array, count, token_axis):
    full_shape = array.shape
    split_shape = (
        full_shape[:token_axis]
        + (count, full_shape[token_axis] // count)
        + full_shape[token_axis + 1 :]
    )
    return jnp.flip(array.reshape(split_shape), axis=token_axis + 1).reshape(full_shape)


def transform(signal):
    seq_parts = lax.axis_size("seq")
    row_count, chan_width = signal.shape
    piece_rows = row_count // seq_parts
    modulus = 2 * row_count * seq_parts
    columns = lax.all_to_all(signal[None], "seq", split_axis=1, concat_axis=0, tiled=True)
    first_cos, first_sin = dft_table(2 * seq_parts, seq_parts, 2 * seq_parts, -1.0)
    real_a = matmul("ka,abw->kbw", first_cos, columns)
    imag_a = matmul("ka,abw->kbw", first_sin, columns)
    freq_index = jnp.arange(2 * seq_parts, dtype=jnp.int32)[:, None]
    row_index = (
        lax.axis_index("seq") * piece_rows + jnp.arange(piece_rows, dtype=jnp.int32)[None, :]
    )
    angles = (freq_index * row_index % modulus).astype(jnp.float32) * (2.0 * math.pi / modulus)
    real_b, imag_b = rotate(real_a, imag_a, angles[:, :, None], -1.0)
    spread = lax.all_to_all(
        jnp.concatenate([real_b, imag_b], axis=2), "seq", split_axis=0, concat_axis=1, tiled=True
    )
    spread_re = spread[:, :, :chan_width]
    spread_im = spread[:, :, chan_width:]
    second_cos, second_sin = dft_table(row_count, row_count, row_count, -1.0)
    out_re = matmul("kb,rbw->rkw", second_cos, spread_re) - matmul(
        "kb,rbw->rkw", second_sin, spread_im
    )
    out_im = matmul("kb,rbw->rkw", second_cos, spread_im) + matmul(
        "kb,rbw->rkw", second_sin, spread_re
    )
    return (out_re, out_im)


def inverse(spec_re, spec_im):
    seq_parts = lax.axis_size("seq")
    row_count = spec_re.shape[1]
    chan_width = spec_re.shape[2]
    modulus = 2 * row_count * seq_parts
    second_cos, second_sin = dft_table(row_count, row_count, row_count, 1.0)
    local_re = matmul("bk,rkw->rbw", second_cos, spec_re) - matmul(
        "bk,rkw->rbw", second_sin, spec_im
    )
    local_im = matmul("bk,rkw->rbw", second_cos, spec_im) + matmul(
        "bk,rkw->rbw", second_sin, spec_re
    )
    freq_index = 2 * lax.axis_index("seq") + jnp.arange(2, dtype=jnp.int32)[:, None]
    row_index = jnp.arange(row_count, dtype=jnp.int32)[None, :]
    angles = (freq_index * row_index % modulus).astype(jnp.float32) * (2.0 * math.pi / modulus)
    turned_re, turned_im = rotate(local_re, local_im, angles[:, :, None], 1.0)
    gathered = lax.all_to_all(
        jnp.concatenate([turned_re, turned_im], axis=2),
        "seq",
        split_axis=1,
        concat_axis=0,
        tiled=True,
    )
    first_cos, first_sin = dft_table(seq_parts, 2 * seq_parts, 2 * seq_parts, 1.0)
    real_rows = matmul("ak,kbw->abw", first_cos, gathered[:, :, :chan_width])
    real_rows = (real_rows - matmul("ak,kbw->abw", first_sin, gathered[:, :, chan_width:])) * (
        1.0 / modulus
    )
    returned = lax.all_to_all(real_rows, "seq", split_axis=0, concat_axis=1, tiled=True)
    return returned[0]


def spectrum(signal):
    return transform(signal)


def restore(spec_re, spec_im):
    return inverse(spec_re, spec_im)


def body(values, gates, filters, skip, cotangent, flagged):
    row_count, chan_width = values.shape
    scale = (row_count * lax.axis_size("seq")) ** (-0.5)
    mirror_bits = lax.axis_size("ch").bit_length() - 1
    chan_axis = 2

    def take(array, index):
        return lax.slice_in_dim(array, index * chan_width, (index + 1) * chan_width, axis=chan_axis)

    def join(pieces):
        return jnp.concatenate(pieces, axis=chan_axis)

    value_rows = values.astype(jnp.float32)
    gate_rows = gates.astype(jnp.float32)
    spec_re, spec_im = spectrum(jnp.concatenate([value_rows, filters], axis=1))
    value_re = take(spec_re, 0)
    value_im = take(spec_im, 0)
    filter_re = take(spec_re, 1)
    filter_im = take(spec_im, 1)
    mirrored = join([filter_re, filter_im])
    for bit_number in range(mirror_bits):
        mirrored = partner(mirrored, "ch", bit_number)
    mirrored = flip_blocks(mirrored, 2, chan_axis)
    twin_re = take(mirrored, 0)
    twin_im = take(mirrored, 1)
    kernel_re = filter_re + twin_re
    kernel_im = filter_im - twin_im
    mixing_re = kernel_re * value_re - kernel_im * value_im
    mixing_im = kernel_re * value_im + kernel_im * value_re
    mixing = restore(mixing_re, mixing_im) + skip[None, :] * value_rows
    mixed = (gate_rows * mixing).astype(jnp.bfloat16)
    masked = cotangent.astype(jnp.float32) * flagged.astype(jnp.float32)[:, None]
    gate_grad = (masked * mixing).astype(jnp.bfloat16)
    inner_grad = gate_rows * masked
    inner_re, inner_im = spectrum(inner_grad)
    prod_re = value_re * inner_re + value_im * inner_im
    prod_im = value_re * inner_im - value_im * inner_re
    mirrored = join([prod_re, prod_im])
    for bit_number in range(mirror_bits):
        mirrored = partner(mirrored, "ch", bit_number)
    mirrored = flip_blocks(mirrored, 2, chan_axis)
    ptwin_re = take(mirrored, 0)
    ptwin_im = take(mirrored, 1)
    grad_re = join([kernel_re * inner_re + kernel_im * inner_im, prod_re + ptwin_re])
    grad_im = join([kernel_re * inner_im - kernel_im * inner_re, prod_im - ptwin_im])
    returned = restore(grad_re, grad_im)
    value_grad = (returned[:, :chan_width] + skip[None, :] * inner_grad).astype(jnp.bfloat16)
    filter_grad = returned[:, chan_width:] * scale
    skip_grad = lax.psum(jnp.sum(value_rows * inner_grad, axis=0), "seq") * scale
    return (mixed, value_grad, gate_grad, filter_grad, skip_grad)


def solution(mesh):
    placed = (P("seq", "ch"), P("seq", "ch"), P("seq", "ch"), P("ch"), P("seq", "ch"), P("seq"))
    return jax.shard_map(
        body,
        mesh=mesh,
        in_specs=placed,
        out_specs=(P("seq", "ch"), P("seq", "ch"), P("seq", "ch"), P("seq", "ch"), P("ch")),
        check_vma=False,
    )
```

profile of v0, /device:TPU:1, one launch (start us, length us, event | category | flops | bytes accessed | tf_op | source)
XLA Modules:
  0.0 997.8 jit_solution(2042080706371923342)
XLA Ops:
  2.8 2.1 copy.31
  4.9 15.6 %all-to-all-start = ((f32[1,256,1024]{2,0,1:T(1,128)}), f32[1,256,1024]{2,0,1:T(1,128)S(1)}, u32[]{:S(2)}, u32[]{:S(2)}) async-start(f32[1,256,1024]{2,0,1:T(1,128)} %copy.31), calls=%async_computation | async-start | bytes 2097152 | tf_op jit(solution)/shard_map/all_to_all | solution.py:45
  22.1 23.1 %all-to-all-done = f32[1,256,1024]{2,0,1:T(1,128)S(1)} async-done(((f32[1,256,1024]{2,0,1:T(1,128)}), f32[1,256,1024]{2,0,1:T(1,128)S(1)}, u32[]{:S(2)}, u32[]{:S(2)}) %all-to-all-start) | async-done | bytes 1048608 | tf_op jit(solution)/shard_map/all_to_all | solution.py:45
  45.3 7.5 all-to-all-start.4
  52.8 2.5 reduce
  55.6 2.4 fusion.24
  58.0 2.8 multiply_subtract_fusion
  61.4 4.7 copy.34
  66.1 3.3 all-to-all-done.4
  69.4 10.1 %all-to-all-start.1 = ((f32[128,4,2048]{2,1,0:T(4,128)}), f32[128,4,2048]{2,1,0:T(4,128)}, u32[]{:S(2)}, u32[]{:S(2)}) async-start(f32[128,4,2048]{2,1,0:T(4,128)} %copy.34), calls=%async_computation.1 | async-start | bytes 8388608 | tf_op jit(solution)/shard_map/all_to_all | solution.py:55
  83.6 2.7 copy.44
  86.3 49.0 %all-to-all-done.1 = f32[128,4,2048]{2,1,0:T(4,128)} async-done(((f32[128,4,2048]{2,1,0:T(4,128)}), f32[128,4,2048]{2,1,0:T(4,128)}, u32[]{:S(2)}, u32[]{:S(2)}) %all-to-all-start.1) | async-done | bytes 4194336 | tf_op jit(solution)/shard_map/all_to_all | solution.py:55
  135.4 48.8 %all-to-all-start.5 = ((f32[128,4,1024]{2,1,0:T(4,128)}), f32[128,4,1024]{2,1,0:T(4,128)}, u32[]{:S(2)}, u32[]{:S(2)}) async-start(f32[128,4,1024]{2,1,0:T(4,128)} %copy.44), calls=%async_computation.5 | async-start | bytes 4194304 | tf_op jit(solution)/shard_map/all_to_all | solution.py:55
  184.2 6.1 copy.35
  190.3 3.5 fusion.235
  193.8 2.7 copy.53
  196.5 4.1 fusion.56
  200.6 4.3 copy.54
  204.9 5.2 subtract_bitcast_fusion.1
  210.1 2.3 copy-done
  212.4 2.9 fusion.54
  215.3 2.9 add_bitcast_fusion.1
  218.3 1.9 slice-done
  220.3 3.2 collective-permute-start
  223.6 55.4 %collective-permute-done = f32[2,256,1024]{1,2,0:T(8,128)} collective-permute-done((f32[2,256,1024]{1,2,0:T(8,128)S(1)}, f32[2,256,1024]{1,2,0:T(8,128)}, u32[]{:S(2)}, u32[]{:S(2)}) %collective-permute-start) | collective-permute-done | bytes 2097184 | tf_op jit(solution)/shard_map/ppermute | solution.py:10
  278.9 3.7 collective-permute-start.1
  282.6 3.5 copy.45
  288.1 2.0 fusion.48
  290.1 3.0 fusion.46
  293.1 2.0 fusion.17
  295.1 78.4 %collective-permute-done.1 = f32[2,256,1024]{1,2,0:T(8,128)} collective-permute-done((f32[2,256,1024]{1,2,0:T(8,128)}, f32[2,256,1024]{1,2,0:T(8,128)}, u32[]{:S(2)}, u32[]{:S(2)}) %collective-permute-start.1) | collective-permute-done | bytes 2097184 | tf_op jit(solution)/shard_map/ppermute | solution.py:10
  373.5 16.8 %rev.7 = f32[2,256,2,512]{1,3,2,0:T(8,128)} reverse(f32[2,256,2,512]{1,3,2,0:T(8,128)} %bitcast.12), dimensions={3} | reverse | bytes 4194304 | tf_op jit(solution)/shard_map/jit(_flip)/rev | solution.py:37
  390.3 6.1 multiply_add_fusion.1
  396.4 1.5 pad_maximum_fusion.5
  399.5 1.4 multiply_subtract_fusion.4
  400.9 2.0 fusion.50
  402.8 2.0 fusion.52
  404.8 2.0 convolution_add_fusion.1
  406.8 2.1 subtract_bitcast_fusion.2
  409.1 2.4 copy.38
  411.5 9.6 all-to-all-start.2
  421.1 24.9 %collective-permute-done.2 = f32[2,256,1024]{1,2,0:T(8,128)} collective-permute-done((f32[2,256,1024]{1,2,0:T(8,128)}, f32[2,256,1024]{1,2,0:T(8,128)}, u32[]{:S(2)}, u32[]{:S(2)}) %collective-permute-start.2) | collective-permute-done | bytes 2097184 | tf_op jit(solution)/shard_map/ppermute | solution.py:10
  446.0 134.9 %collective-permute-done.3 = f32[2,256,1024]{1,2,0:T(8,128)S(1)} collective-permute-done((f32[2,256,1024]{1,2,0:T(8,128)}, f32[2,256,1024]{1,2,0:T(8,128)S(1)}, u32[]{:S(2)}, u32[]{:S(2)}) %collective-permute-start.3) | collective-permute-done | bytes 2097184 | tf_op jit(solution)/shard_map/ppermute | solution.py:10
  582.2 16.9 %rev.8 = f32[2,256,2,512]{1,3,2,0:T(8,128)} reverse(f32[2,256,2,512]{1,3,2,0:T(8,128)} %bitcast.123), dimensions={3} | reverse | bytes 4194304 | tf_op jit(solution)/shard_map/jit(_flip)/rev | solution.py:37
  599.2 1.9 slice_add_fusion
  601.1 2.8 fusion.4
  604.0 2.8 fusion.5
  606.8 2.9 fusion.8
  609.7 3.5 subtract_bitcast_fusion
  613.2 2.3 pad_maximum_fusion.1
  615.5 7.3 copy.48
  622.8 10.5 %all-to-all-start.6 = ((f32[2,256,2048]{2,0,1:T(2,128)}), f32[2,256,2048]{2,0,1:T(2,128)}, u32[]{:S(2)}, u32[]{:S(2)}) async-start(f32[2,256,2048]{2,0,1:T(2,128)} %copy.48), calls=%async_computation.6 | async-start | bytes 8388608 | tf_op jit(solution)/shard_map/all_to_all | solution.py:86
  633.3 3.8 copy.39
  637.1 2.7 all_to_all.93
  642.5 89.7 %all-to-all-done.6 = f32[2,256,2048]{2,0,1:T(2,128)} async-done(((f32[2,256,2048]{2,0,1:T(2,128)}), f32[2,256,2048]{2,0,1:T(2,128)}, u32[]{:S(2)}, u32[]{:S(2)}) %all-to-all-start.6) | async-done | bytes 4194336 | tf_op jit(solution)/shard_map/all_to_all | solution.py:86
  732.2 6.7 all-to-all-start.3
  738.9 6.7 copy.49
  745.7 6.2 all_to_all.104
  751.8 2.9 fusion
  754.7 2.9 fusion.13
  757.7 1.7 copy.50
  759.3 12.7 %all-to-all-start.7 = ((f32[64,4,1024]{2,1,0:T(4,128)}), f32[64,4,1024]{2,1,0:T(4,128)S(1)}, u32[]{:S(2)}, u32[]{:S(2)}) async-start(f32[64,4,1024]{2,1,0:T(4,128)} %copy.50), calls=%async_computation.7 | async-start | bytes 2097152 | tf_op jit(solution)/shard_map/all_to_all | solution.py:98
  772.3 22.1 %all-to-all-done.7 = f32[64,4,1024]{2,1,0:T(4,128)S(1)} async-done(((f32[64,4,1024]{2,1,0:T(4,128)}), f32[64,4,1024]{2,1,0:T(4,128)S(1)}, u32[]{:S(2)}, u32[]{:S(2)}) %all-to-all-start.7) | async-done | bytes 1048608 | tf_op jit(solution)/shard_map/all_to_all | solution.py:98
  796.2 200.9 %psum.7 = f32[512]{0:T(512)S(1)} all-reduce(f32[512]{0:T(512)S(1)} %get-tuple-element.35), channel_id=1, replica_groups=mesh['seq'=64,'ch'=4] {'seq'}, use_global_device_ids=true, to_apply=%region_1.2 | all-reduce | flops 512 | bytes 4096 | tf_op jit(solution)/shard_map/psum | solution.py:158
  (72 shorter events, 19.2 us)
Async XLA Ops:
  2.8 17.7 %copy-start.18 = (s32[256]{0:T(256)S(1)}, s32[256]{0:T(256)}, u32[]{:S(2)}) copy-start(s32[256]{0:T(256)} %param.11) | copy-start | bytes 3076
  2.8 17.7 %copy-start.13 = (bf16[256,512]{1,0:T(8,128)(2,1)S(1)}, bf16[256,512]{1,0:T(8,128)(2,1)}, u32[]{:S(2)}) copy-start(bf16[256,512]{1,0:T(8,128)(2,1)} %param.10) | copy-start | bytes 786436
  2.8 17.7 %copy-start.14 = (bf16[256,512]{1,0:T(8,128)(2,1)S(1)}, bf16[256,512]{1,0:T(8,128)(2,1)}, u32[]{:S(2)}) copy-start(bf16[256,512]{1,0:T(8,128)(2,1)} %param.7) | copy-start | bytes 786436
  4.9 40.4 %all-to-all-start = ((f32[1,256,1024]{2,0,1:T(1,128)}), f32[1,256,1024]{2,0,1:T(1,128)S(1)}, u32[]{:S(2)}, u32[]{:S(2)}) async-start(f32[1,256,1024]{2,0,1:T(1,128)} %copy.31), calls=%async_computation | async-start | bytes 2097152 | tf_op jit(solution)/shard_map/all_to_all | solution.py:45
  45.3 24.1 %all-to-all-start.4 = ((f32[1,256,512]{2,0,1:T(1,128)}), f32[1,256,512]{2,0,1:T(1,128)S(1)}, u32[]{:S(2)}, u32[]{:S(2)}) async-start(f32[1,256,512]{2,0,1:T(1,128)} %copy.41), calls=%async_computation.4 | async-start | bytes 1048576 | tf_op jit(solution)/shard_map/all_to_all | solution.py:45
  69.4 66.0 %all-to-all-start.1 = ((f32[128,4,2048]{2,1,0:T(4,128)}), f32[128,4,2048]{2,1,0:T(4,128)}, u32[]{:S(2)}, u32[]{:S(2)}) async-start(f32[128,4,2048]{2,1,0:T(4,128)} %copy.34), calls=%async_computation.1 | async-start | bytes 8388608 | tf_op jit(solution)/shard_map/all_to_all | solution.py:55
  135.4 147.3 %all-to-all-start.5 = ((f32[128,4,1024]{2,1,0:T(4,128)}), f32[128,4,1024]{2,1,0:T(4,128)}, u32[]{:S(2)}, u32[]{:S(2)}) async-start(f32[128,4,1024]{2,1,0:T(4,128)} %copy.44), calls=%async_computation.5 | async-start | bytes 4194304 | tf_op jit(solution)/shard_map/all_to_all | solution.py:55
  210.1 5.2 copy-start.1
  210.1 2.3 copy-start
  218.2 2.1 copy-start.3
  218.2 2.0 slice-start
  220.3 58.6 %collective-permute-start = (f32[2,256,1024]{1,2,0:T(8,128)S(1)}, f32[2,256,1024]{1,2,0:T(8,128)}, u32[]{:S(2)}, u32[]{:S(2)}) collective-permute-start(f32[2,256,1024]{1,2,0:T(8,128)S(1)} %pad_maximum_fusion.2), channel_id=1, source_target_pairs={{0,1},{1,0},{2,3},{3,2},{4,5},{5,4},{6,7},{7,6},{8,9},{9,8},{10,11... | collective-permute-start | bytes 6291464 | tf_op jit(solution)/shard_map/ppermute | solution.py:10
  278.9 94.6 %collective-permute-start.1 = (f32[2,256,1024]{1,2,0:T(8,128)}, f32[2,256,1024]{1,2,0:T(8,128)}, u32[]{:S(2)}, u32[]{:S(2)}) collective-permute-start(f32[2,256,1024]{1,2,0:T(8,128)} %collective-permute-done), channel_id=1, source_target_pairs={{0,2},{1,3},{2,0},{3,1},{4,6},{5,7},{6,4},{7,5},{8,10},{9,11},{10,... | collective-permute-start | bytes 6291464 | tf_op jit(solution)/shard_map/ppermute | solution.py:10
  287.5 2.6 copy-start.6
  373.5 16.8 %copy-start.2 = (f32[2,256,1024]{1,2,0:T(8,128)S(1)}, f32[2,256,1024]{1,2,0:T(8,128)}, u32[]{:S(2)}) copy-start(f32[2,256,1024]{1,2,0:T(8,128)} %copy-done.1) | copy-start | bytes 6291460
  396.4 1.7 copy-start.7
  396.4 2.1 copy-start.9
  396.4 3.1 copy-start.4
  398.5 47.5 %collective-permute-start.2 = (f32[2,256,1024]{1,2,0:T(8,128)}, f32[2,256,1024]{1,2,0:T(8,128)}, u32[]{:S(2)}, u32[]{:S(2)}) collective-permute-start(f32[2,256,1024]{1,2,0:T(8,128)} %pad_maximum_fusion.5), channel_id=1, source_target_pairs={{0,1},{1,0},{2,3},{3,2},{4,5},{5,4},{6,7},{7,6},{8,9},{9,8},{10,11... | collective-permute-start | bytes 6291464 | tf_op jit(solution)/shard_map/ppermute | solution.py:10
  411.5 211.3 %all-to-all-start.2 = ((f32[2,256,1024]{2,0,1:T(2,128)}), f32[2,256,1024]{2,0,1:T(2,128)}, u32[]{:S(2)}, u32[]{:S(2)}) async-start(f32[2,256,1024]{2,0,1:T(2,128)} %copy.38), calls=%async_computation.2 | async-start | bytes 4194304 | tf_op jit(solution)/shard_map/all_to_all | solution.py:86
  446.0 134.9 %collective-permute-start.3 = (f32[2,256,1024]{1,2,0:T(8,128)}, f32[2,256,1024]{1,2,0:T(8,128)S(1)}, u32[]{:S(2)}, u32[]{:S(2)}) collective-permute-start(f32[2,256,1024]{1,2,0:T(8,128)} %collective-permute-done.2), channel_id=1, source_target_pairs={{0,2},{1,3},{2,0},{3,1},{4,6},{5,7},{6,4},{7,5},{8,10},{9,11},{10,... | collective-permute-start | bytes 6291464 | tf_op jit(solution)/shard_map/ppermute | solution.py:10
  580.9 1.3 copy-start.12
  582.2 16.9 %copy-start.8 = (f32[2,256,512]{1,2,0:T(8,128)S(1)}, f32[2,256,512]{1,2,0:T(8,128)}, u32[]{:S(2)}) copy-start(f32[2,256,512]{1,2,0:T(8,128)} %copy-done.7) | copy-start | bytes 3145732
  582.2 16.9 %copy-start.10 = (f32[2,256,512]{1,2,0:T(8,128)S(1)}, f32[2,256,512]{1,2,0:T(8,128)}, u32[]{:S(2)}) copy-start(f32[2,256,512]{1,2,0:T(8,128)} %copy-done.9) | copy-start | bytes 3145732
  599.2 1.9 copy-start.11
  603.9 2.9 copy-start.5
  622.8 109.4 %all-to-all-start.6 = ((f32[2,256,2048]{2,0,1:T(2,128)}), f32[2,256,2048]{2,0,1:T(2,128)}, u32[]{:S(2)}, u32[]{:S(2)}) async-start(f32[2,256,2048]{2,0,1:T(2,128)} %copy.48), calls=%async_computation.6 | async-start | bytes 8388608 | tf_op jit(solution)/shard_map/all_to_all | solution.py:86
  732.2 27.1 %all-to-all-start.3 = ((f32[64,4,512]{2,1,0:T(4,128)}), f32[64,4,512]{2,1,0:T(4,128)S(1)}, u32[]{:S(2)}, u32[]{:S(2)}) async-start(f32[64,4,512]{2,1,0:T(4,128)} %copy.40), calls=%async_computation.3 | async-start | bytes 1048576 | tf_op jit(solution)/shard_map/all_to_all | solution.py:98
  759.3 35.1 %all-to-all-start.7 = ((f32[64,4,1024]{2,1,0:T(4,128)}), f32[64,4,1024]{2,1,0:T(4,128)S(1)}, u32[]{:S(2)}, u32[]{:S(2)}) async-start(f32[64,4,1024]{2,1,0:T(4,128)} %copy.50), calls=%async_computation.7 | async-start | bytes 2097152 | tf_op jit(solution)/shard_map/all_to_all | solution.py:98
  772.1 22.7 %copy-start.15 = (bf16[256,512]{1,0:T(8,128)(2,1)S(1)}, bf16[256,512]{1,0:T(8,128)(2,1)}, u32[]{:S(2)}) copy-start(bf16[256,512]{1,0:T(8,128)(2,1)} %param.7) | copy-start | bytes 786436
  772.1 22.7 %copy-start.16 = (bf16[256,512]{1,0:T(8,128)(2,1)S(1)}, bf16[256,512]{1,0:T(8,128)(2,1)}, u32[]{:S(2)}) copy-start(bf16[256,512]{1,0:T(8,128)(2,1)} %param.6) | copy-start | bytes 786436
  772.1 22.7 %copy-start.17 = (f32[512]{0:T(512)S(1)}, f32[512]{0:T(512)}, u32[]{:S(2)}) copy-start(f32[512]{0:T(512)} %param.9) | copy-start | bytes 6148
where the time goes:
time: 1000 us; the launch traced here: 998 us
  waiting for transfers between devices  481 us (48%)
  blocking collectives  201 us (20%)
  starting transfers between devices  129 us (13%)
  local copies, waits for them, and re-layouts  106 us (11%)
  matrix products  63.3 us (6%)
  other arithmetic  16.2 us (2%)
    ppermute x4, waiting for transfers between devices, partner(): lax.ppermute(array, axis, [(i, i ^ 1 << apart) for i in range(lax.axis_si...  294 us
    psum x1, blocking collectives, body(): lax.psum(jnp.sum(value_rows * inner_grad, axis=0), 'seq') * scale  201 us
    all_to_all x2, waiting for transfers between devices, inverse(): lax.all_to_all(jnp.concatenate([turned_re, turned_im], axis=2), 'seq', sp...  89.7 us
    dot_general x24, matrix products, matmul(): return jnp.einsum(form, left, right, precision=lax.Precision.HIGHEST)  63.3 us
    all_to_all x2, starting transfers between devices, transform(): lax.all_to_all(jnp.concatenate([real_b, imag_b], axis=2), 'seq', split_ax...  58.9 us
    all_to_all x2, waiting for transfers between devices, transform(): lax.all_to_all(jnp.concatenate([real_b, imag_b], axis=2), 'seq', split_ax...  49 us
    rev x2, local copies, waits for them, and re-layouts, flip_blocks(): jnp.flip(array.reshape(split_shape), axis=token_axis + 1)  33.7 us
    all_to_all x2, waiting for transfers between devices, transform(): lax.all_to_all(signal[None], 'seq', split_axis=1, concat_axis=0, tiled=True)  26.4 us
  transfers between devices with their start and end apart: 12, of which 9 were waited for; matrix products, arithmetic and copies ran while one was open for 14% of the time, Pallas kernels for 0%

commit v1 on v0

v1 whole, which is shorter than its diff:
```python
import functools
import math

import jax
import jax.numpy as jnp
import ml_dtypes
import numpy as np
from jax import lax
from jax.experimental import pallas as pl
from jax.experimental.pallas import tpu as pltpu
from jax.sharding import PartitionSpec as P

MESH = pl.DeviceIdType.MESH
F32 = jnp.float32
BF16 = jnp.bfloat16
SEQ = 64
SIDE = 128
GROUPS = 128


def halves(table):
    high = table.astype(ml_dtypes.bfloat16)
    low = (table - high.astype(np.float64)).astype(ml_dtypes.bfloat16)
    return high, low


def tables():
    freq = np.arange(SIDE)
    coarse = np.arange(SIDE)
    order = np.concatenate([2 * np.arange(SEQ), 2 * np.arange(SEQ) + 1])
    angle = 2 * math.pi * ((2 * freq[:, None] + 1) * order[None, :] % 512) / 512
    first = np.concatenate([np.cos(angle), -np.sin(angle)], axis=0)
    first_hi, first_lo = halves(first)
    first_in = np.concatenate([first_hi, first_hi, first_lo], axis=1)
    last_hi, last_lo = halves(first.T * 2.0**-14)
    last_out = np.concatenate([last_hi, last_hi, last_lo], axis=1)
    turn = 2 * math.pi * ((2 * freq[:, None] + 1) * coarse[None, :]) / 65536
    angle = 2 * math.pi * (coarse[:, None] * coarse[None, :] % SIDE) / SIDE
    cosine, sine = np.cos(angle), np.sin(angle)
    second = np.block([[cosine, -sine], [sine, cosine]])
    second_in = np.concatenate([halves(second)[0]] * 2 + [halves(second)[1]], axis=0)
    second_out = np.concatenate([halves(second.T)[0]] * 2 + [halves(second.T)[1]], axis=0)
    return (
        first_in,
        last_out,
        np.cos(turn).astype(np.float32),
        np.sin(turn).astype(np.float32),
        second_in,
        second_out,
    )


def split(array):
    high = array.astype(BF16)
    return high, (array - high.astype(F32)).astype(BF16)


def dot(left, right):
    return jnp.dot(left, right, preferred_element_type=F32)


def second_step(parts, table):
    high, low = split(jnp.concatenate(parts, axis=0))
    return dot(jnp.concatenate([high, low, high], axis=1), table)


def rotate(both, cosine, sine):
    turned = []
    for side in range(2):
        real = both[:SIDE, side * SIDE : (side + 1) * SIDE]
        imag = both[SIDE:, side * SIDE : (side + 1) * SIDE]
        turned.append(
            jnp.concatenate([real * cosine + imag * sine, imag * cosine - real * sine], axis=1)
        )
    return turned


def rotate_back(both, cosine, sine):
    real, imag = both[:, :SIDE], both[:, SIDE:]
    return real * cosine - imag * sine, imag * cosine + real * sine


def times(left, right):
    lr, li, rr, ri = left[:, :SIDE], left[:, SIDE:], right[:, :SIDE], right[:, SIDE:]
    return jnp.concatenate([lr * rr - li * ri, lr * ri + li * rr], axis=1)


def conj_times(left, right):
    lr, li, rr, ri = left[:, :SIDE], left[:, SIDE:], right[:, :SIDE], right[:, SIDE:]
    return jnp.concatenate([lr * rr + li * ri, lr * ri - li * rr], axis=1)


def add_conj(left, right):
    return jnp.concatenate(
        [left[:, :SIDE] + right[:, :SIDE], left[:, SIDE:] - right[:, SIDE:]], axis=1
    )


def conj(array):
    return jnp.concatenate([array[:, :SIDE], -array[:, SIDE:]], axis=1)


def kernel(
    values, gates, filters, skip, cotangent, flagged,
    first_in, last_out, cosine, sine, second_in, second_out,
    mixed, value_grad, gate_grad, filter_grad, skip_grad,
    send_fv, send_w, recv_fv, recv_w,
    back_mix, back_vg, back_fg, back_skip,
    ret_mix, ret_vg, ret_fg, ret_skip,
    inner, kept_k, kept_v, send_sem, recv_sem,
):
    seq = lax.axis_index("seq")
    ch = lax.axis_index("ch")
    outer = (ch == 0) | (ch == 3)
    mirror = ch // 2

    owner_ch = [jnp.where(outer, 1, 0), jnp.where(outer, 2, 3)]
    group_sign = 1 - 2 * mirror
    group_base = 127 * mirror
    home_ch = [jnp.where(outer, 1, 0), jnp.where(outer, 2, 3)]
    mine = seq + SEQ * mirror

    x, y, rest = seq // 16, seq // 4 % 4, seq % 4
    along_x = [(x + step) % 4 * 16 for step in range(4)]
    along_y = [(y + step) % 4 * 4 for step in range(4)]

    def peers(visit):
        def some(step, carry):
            half = step % 2
            there = (rest + step // 2) % 4
            for px in along_x:
                for py in along_y:
                    visit(px + py + there, half)
            return carry

        lax.fori_loop(0, 8, some, 0)

    barrier = pltpu.get_barrier_semaphore()

    def greet(there, half):
        pl.semaphore_signal(
            barrier,
            inc=1,
            device_id=(there, jnp.where(half == 0, owner_ch[0], owner_ch[1])),
            device_id_type=MESH,
        )

    peers(greet)

    def to_owner(src, dst, which):
        def visit(there, half):
            group = group_base + group_sign * (half * SEQ + there)
            pltpu.make_async_remote_copy(
                src_ref=src.at[group // 2, group % 2],
                dst_ref=dst.at[mirror * SEQ + seq],
                send_sem=send_sem.at[which],
                recv_sem=recv_sem.at[which],
                device_id=(there, jnp.where(half == 0, owner_ch[0], owner_ch[1])),
                device_id_type=MESH,
            ).start()

        peers(visit)

    def to_home(src, dst, which):
        def visit(there, half):
            group = jnp.where(half == 0, mine, 127 - mine)
            pltpu.make_async_remote_copy(
                src_ref=src.at[half * SEQ + there],
                dst_ref=dst.at[group // 2, group % 2],
                send_sem=send_sem.at[which],
                recv_sem=recv_sem.at[which],
                device_id=(there, jnp.where(half == 0, home_ch[0], home_ch[1])),
                device_id_type=MESH,
            ).start()

        peers(visit)

    def skips_home(which):
        def visit(there, half):
            group = jnp.where(half == 0, mine, 127 - mine)
            pltpu.make_async_remote_copy(
                src_ref=back_skip.at[half],
                dst_ref=ret_skip.at[group],
                send_sem=send_sem.at[which],
                recv_sem=recv_sem.at[which],
                device_id=(there, jnp.where(half == 0, home_ch[0], home_ch[1])),
                device_id_type=MESH,
            ).start()

        peers(visit)

    def wait_for(semaphores, which, ref):
        pltpu.make_async_copy(ref, ref, semaphores.at[which]).wait()

    rows = lax.broadcasted_iota(jnp.int32, (16, 8, SIDE), 1) < 4

    def block(half, part):
        return pl.ds(half * SIDE, SIDE), pl.ds(part * SIDE, SIDE)

    def pack(top, bottom):
        top, bottom = top.reshape(16, 8, SIDE), bottom.reshape(16, 8, SIDE)
        even = jnp.where(rows, top, pltpu.roll(bottom, 4, 1))
        odd = jnp.where(rows, pltpu.roll(top, 4, 1), bottom)
        return even, odd

    def unpack(even, odd):
        top = jnp.where(rows, even, pltpu.roll(odd, 4, 1))
        bottom = jnp.where(rows, pltpu.roll(even, 4, 1), odd)
        return top.reshape(SIDE, SIDE), bottom.reshape(SIDE, SIDE)

    flags = [
        jnp.broadcast_to(flagged[half : half + 1, :].astype(F32), (SIDE, SIDE)).T
        for half in range(2)
    ]

    for part in range(4):
        here = pl.ds(part * 16, 16)
        for which, source in enumerate((filters, values)):
            turned = [source[block(half, part)].astype(F32).T for half in range(2)]
            send_fv[here, 0, which], send_fv[here, 1, which] = pack(*turned)
    for part in range(4):
        here = pl.ds(part * 16, 16)
        turned = []
        for half in range(2):
            at = block(half, part)
            product = gates[at].astype(F32) * (cotangent[at].astype(F32) * flags[half])
            inner[at] = product
            turned.append(product.T)
        send_w[here, 0], send_w[here, 1] = pack(*turned)

    pl.semaphore_wait(barrier, 128)
    to_owner(send_fv, recv_fv, 0)
    to_owner(send_w, recv_w, 1)

    cos_turn, sin_turn = cosine[...], sine[...]

    def load(flat, start, stride):
        return jnp.concatenate(
            [flat[pl.ds(start + 4 * half, SEQ, stride=stride), :] for half in range(2)], axis=0
        )

    def load_pair(ref, which, count, pair):
        flat = ref.reshape(2 * SEQ * count * 8, SIDE)
        stride = count * 8
        first = load(flat, which * 8 + pair, stride)
        second = load(flat, SEQ * stride + which * 8 + 3 - pair, stride)
        return jnp.concatenate([first, second], axis=1)

    def store_pair(ref, pair, result):
        flat = ref.reshape(2 * SEQ * 8, SIDE)
        for half in range(2):
            top = result[half * SEQ : (half + 1) * SEQ]
            flat[pl.ds(4 * half + pair, SEQ, stride=8), :] = top[:, :SIDE]
            flat[pl.ds(SEQ * 8 + 4 * half + 3 - pair, SEQ, stride=8), :] = top[:, SIDE:]

    def first_step(signal):
        high, low = split(signal)
        return dot(first_in[...], jnp.concatenate([high, low, high], axis=0))

    def first_step_exact(signal):
        high = signal.astype(BF16)
        return dot(first_in[:, SIDE:], jnp.concatenate([high, high], axis=0))

    def inverse(first, second):
        both = second_step([first, second], second_out[...])
        r0, i0 = rotate_back(both[:SIDE], cos_turn, sin_turn)
        r1, i1 = rotate_back(both[SIDE:], cos_turn, sin_turn)
        stacked = jnp.concatenate(
            [jnp.concatenate([r0, r1], axis=1), jnp.concatenate([i0, i1], axis=1)], axis=0
        )
        high, low = split(stacked)
        return dot(last_out[...], jnp.concatenate([high, low, high], axis=0))

    wait_for(recv_sem, 0, recv_fv)
    for pair in range(4):
        f_parts = rotate(first_step(load_pair(recv_fv, 0, 2, pair)), cos_turn, sin_turn)
        v_parts = rotate(first_step_exact(load_pair(recv_fv, 1, 2, pair)), cos_turn, sin_turn)
        spectra = second_step(f_parts + v_parts, second_in[...])
        f0, f1, v0, v1 = (spectra[i * SIDE : (i + 1) * SIDE] for i in range(4))
        k = add_conj(f0, f1)
        kept_k[pair] = k
        kept_v[pair, 0] = v0
        kept_v[pair, 1] = v1
        store_pair(back_mix, pair, inverse(times(k, v0), conj_times(k, v1)))
    to_home(back_mix, ret_mix, 2)

    wait_for(recv_sem, 1, recv_w)
    lanes = lax.broadcasted_iota(jnp.int32, (1, SIDE), 1)
    skip_rows = [jnp.zeros((1, SIDE), F32), jnp.zeros((1, SIDE), F32)]
    for pair in range(4):
        signal = load_pair(recv_w, 0, 1, pair)
        sums = jnp.sum(signal * load_pair(recv_fv, 1, 2, pair), axis=0, keepdims=True)
        for side, group, row in ((0, mine, pair), (1, 127 - mine, 3 - pair)):
            total = jnp.sum(sums[:, side * SIDE : (side + 1) * SIDE], axis=1, keepdims=True)
            skip_rows[side] += jnp.where(lanes == group % 32 * 4 + row, total, 0.0)
        spectra = second_step(rotate(first_step(signal), cos_turn, sin_turn), second_in[...])
        w0, w1 = spectra[:SIDE], spectra[SIDE:]
        k = kept_k[pair]
        store_pair(back_vg, pair, inverse(conj_times(k, w0), times(k, w1)))
        product = add_conj(conj_times(kept_v[pair, 0], w0), conj_times(kept_v[pair, 1], w1))
        store_pair(back_fg, pair, inverse(product, conj(product)))
    back_skip[0] = skip_rows[0]
    back_skip[1] = skip_rows[1]
    to_home(back_vg, ret_vg, 3)
    to_home(back_fg, ret_fg, 4)
    skips_home(5)

    def returned(ref, part):
        here = pl.ds(part * 16, 16)
        top, bottom = unpack(ref[here, 0], ref[here, 1])
        return top.T, bottom.T

    wait_for(recv_sem, 2, ret_mix)
    for part in range(4):
        for half, result in enumerate(returned(ret_mix, part)):
            at = block(half, part)
            result = result + skip[:, at[1]] * values[at].astype(F32)
            mixed[at] = (gates[at].astype(F32) * result).astype(BF16)
            gate_grad[at] = (cotangent[at].astype(F32) * flags[half] * result).astype(BF16)
    wait_for(recv_sem, 3, ret_vg)
    for part in range(4):
        for half, result in enumerate(returned(ret_vg, part)):
            at = block(half, part)
            value_grad[at] = (result + skip[:, at[1]] * inner[at]).astype(BF16)
    wait_for(recv_sem, 4, ret_fg)
    for part in range(4):
        for half, result in enumerate(returned(ret_fg, part)):
            filter_grad[block(half, part)] = result * 2.0**-7
    wait_for(recv_sem, 5, ret_skip)
    for part in range(4):
        skip_grad[part : part + 1, :] = jnp.sum(ret_skip[pl.ds(part * 32, 32)], axis=0) * 2.0**-7

    for which, ref in enumerate((recv_fv, recv_w, ret_mix, ret_vg, ret_fg, ret_skip)):
        wait_for(send_sem, which, ref)


def body(values, gates, filters, skip, cotangent, flagged):
    constants = [jnp.asarray(table) for table in tables()]
    bases, width = values.shape
    vmem = pl.BlockSpec(memory_space=pltpu.VMEM)

    def scratch(*shape):
        return pltpu.VMEM(shape, F32)

    outs = pl.pallas_call(
        kernel,
        out_shape=[
            jax.ShapeDtypeStruct((bases, width), BF16),
            jax.ShapeDtypeStruct((bases, width), BF16),
            jax.ShapeDtypeStruct((bases, width), BF16),
            jax.ShapeDtypeStruct((bases, width), F32),
            jax.ShapeDtypeStruct((4, SIDE), F32),
        ],
        in_specs=[vmem] * 12,
        out_specs=[vmem] * 5,
        scratch_shapes=[
            scratch(64, 2, 2, 8, SIDE),
            scratch(64, 2, 8, SIDE),
            scratch(GROUPS, 2, 8, SIDE),
            scratch(GROUPS, 8, SIDE),
            scratch(GROUPS, 8, SIDE),
            scratch(GROUPS, 8, SIDE),
            scratch(GROUPS, 8, SIDE),
            scratch(2, 1, SIDE),
            scratch(64, 2, 8, SIDE),
            scratch(64, 2, 8, SIDE),
            scratch(64, 2, 8, SIDE),
            scratch(GROUPS, 1, SIDE),
            scratch(bases, width),
            scratch(4, SIDE, 2 * SIDE),
            scratch(4, 2, SIDE, 2 * SIDE),
            pltpu.SemaphoreType.DMA((6,)),
            pltpu.SemaphoreType.DMA((6,)),
        ],
        compiler_params=pltpu.CompilerParams(
            collective_id=0, has_side_effects=True, vmem_limit_bytes=48 << 20
        ),
        name="hyena",
    )(values, gates, filters, skip.reshape(1, width), cotangent, flagged.reshape(2, SIDE), *constants)
    return (*outs[:4], outs[4].reshape(width))


def solution(mesh):
    placed = (P("seq", "ch"), P("seq", "ch"), P("seq", "ch"), P("ch"), P("seq", "ch"), P("seq"))
    return jax.shard_map(
        body,
        mesh=mesh,
        in_specs=placed,
        out_specs=(P("seq", "ch"), P("seq", "ch"), P("seq", "ch"), P("seq", "ch"), P("ch")),
        check_vma=False,
    )
```

time: 1000 us -> 101 us (0.10)
  waiting for transfers between devices: 481 us -> 0 us
  blocking collectives: 201 us -> 0 us
  starting transfers between devices: 129 us -> 0 us
  local copies, waits for them, and re-layouts: 106 us -> 13.6 us
  Pallas kernels: 0 us -> 86.3 us
  matrix products: 63.3 us -> 0 us
  other arithmetic: 16.2 us -> 0 us
    ppermute x4 -> x0, waiting for transfers between devices: 294 us -> none  [partner(): lax.ppermute(array, axis, [(i, i ^ 1 << apart) for i in range(lax.axis_si...]
    psum x1 -> x0, blocking collectives: 201 us -> none  [body(): lax.psum(jnp.sum(value_rows * inner_grad, axis=0), 'seq') * scale]
    all_to_all x8 -> x0, waiting for transfers between devices: 187 us -> none  [the longest x2 89.7 us: inverse(): lax.all_to_all(jnp.concatenate([turned_re, turned_im], axis=2), 'seq', sp...]
    all_to_all x8 -> x0, starting transfers between devices: 122 us -> none  [the longest x2 58.9 us: transform(): lax.all_to_all(jnp.concatenate([real_b, imag_b], axis=2), 'seq', split_ax...]
    pallas_call x0 -> x1, Pallas kernels: none -> 86.3 us  [body(): pl.pallas_call(kernel, out_shape=[jax.ShapeDtypeStruct((bases, width), BF...]
    dot_general x24 -> x0, matrix products: 63.3 us -> none  [matmul(): return jnp.einsum(form, left, right, precision=lax.Precision.HIGHEST)]
    rev x2 -> x0, local copies, waits for them, and re-layouts: 33.7 us -> none  [flip_blocks(): jnp.flip(array.reshape(split_shape), axis=token_axis + 1)]
    all_to_all x8 -> x0, local copies, waits for them, and re-layouts: 29.4 us -> none  [the longest x4 19.3 us: inverse(): lax.all_to_all(jnp.concatenate([turned_re, turned_im], axis=2), 'seq', sp...]
  transfers between devices with their start and end apart: 12 -> 0, of which waited for: 9 -> 0; matrix products, arithmetic and copies ran while one was open for 14% -> 0% of each run, Pallas kernels for 0% -> 0%
where the time goes in v1:
time: 101 us
  Pallas kernels  86.3 us (85%)
  local copies, waits for them, and re-layouts  13.6 us (13%)
    pallas_call x1, Pallas kernels, body(): pl.pallas_call(kernel, out_shape=[jax.ShapeDtypeStruct((bases, width), BF...  86.3 us
    unnamed x29, local copies, waits for them, and re-layouts  13.6 us

profile of v1, /device:TPU:1, one launch (start us, length us, event | category | flops | bytes accessed | tf_op | source)
XLA Modules:
  0.0 100.5 jit_solution(1926943057322082180)
XLA Ops:
  0.6 0.0 copy-start.10
  0.6 0.0 copy-start.11
  0.7 0.7 copy-done.10
  1.3 0.0 copy-done.11
  1.3 0.0 copy-start
  1.3 1.0 %copy-done = f32[256,512]{1,0:T(8,128)S(1)} copy-done((f32[256,512]{1,0:T(8,128)S(1)}, f32[256,512]{1,0:T(8,128)}, u32[]{:S(2)}) %copy-start) | copy-done | bytes 524312
  2.4 0.0 copy-start.1
  2.4 1.0 copy-done.1
  3.4 0.0 copy-start.2
  3.4 1.0 copy-done.2
  4.4 0.0 copy-start.3
  4.4 0.9 copy-done.3
  5.3 0.0 copy-start.4
  5.3 0.9 copy-done.4
  6.3 0.0 copy-start.5
  6.3 0.9 copy-done.5
  7.2 0.0 copy-start.6
  7.2 0.9 copy-done.6
  8.1 0.0 copy-start.7
  8.1 0.9 copy-done.7
  9.1 0.0 copy-start.8
  9.1 0.8 copy-done.8
  9.9 0.0 copy-start.9
  9.9 0.8 copy-done.9
  10.8 86.3 %hyena.1 = (bf16[256,512]{1,0:T(8,128)(2,1)S(1)}, bf16[256,512]{1,0:T(8,128)(2,1)S(1)}, bf16[256,512]{1,0:T(8,128)(2,1)S(1)}, f32[256,512]{1,0:T(8,128)S(1)}, f32[4,128]{1,0:T(4,128)S(1)}) custom-call(bf16[256,512]{1,0:T(8,128)(2,1)S(1)} %copy-done.3, bf16[256,512]{1,0:T(8,128)(2,1)S(1)} %copy-done.4, f32[256,512]{1,0:T(8,128)S(1)} %copy-done, ...), custom_call_target="tpu_custom_call" | custom-call | tf_op jit(solution)/shard_map/hyena/pallas_call | solution.py:345
  97.0 0.7 copy.22
  97.7 0.7 copy.23
  98.4 0.7 copy.24
  99.1 0.8 copy.25
  99.9 0.6 copy.26
Async XLA Ops:
  0.6 0.7 copy-start.10
  0.6 0.7 copy-start.11
  1.3 1.0 %copy-start = (f32[256,512]{1,0:T(8,128)S(1)}, f32[256,512]{1,0:T(8,128)}, u32[]{:S(2)}) copy-start(f32[256,512]{1,0:T(8,128)} %filters.1) | copy-start | bytes 1572868
  2.4 1.0 copy-start.1
  3.4 1.0 copy-start.2
  4.4 0.9 copy-start.3
  5.3 0.9 copy-start.4
  6.3 0.9 copy-start.5
  7.2 0.9 copy-start.6
  8.1 0.9 copy-start.7
  9.1 0.8 copy-start.8
  9.9 0.8 copy-start.9

commit v2 on v1

v2 whole, which is shorter than its diff:
```python
import functools
import math

import jax
import jax.numpy as jnp
import ml_dtypes
import numpy as np
from jax import lax
from jax.experimental import pallas as pl
from jax.experimental.pallas import tpu as pltpu
from jax.sharding import PartitionSpec as P

MESH = pl.DeviceIdType.MESH
F32 = jnp.float32
BF16 = jnp.bfloat16
SEQ = 64
SIDE = 128
GROUPS = 128


def halves(table):
    high = table.astype(ml_dtypes.bfloat16)
    low = (table - high.astype(np.float64)).astype(ml_dtypes.bfloat16)
    return high, low


def tables():
    freq = np.arange(SIDE)
    coarse = np.arange(SIDE)
    order = np.concatenate([2 * np.arange(SEQ), 2 * np.arange(SEQ) + 1])
    angle = 2 * math.pi * ((2 * freq[:, None] + 1) * order[None, :] % 512) / 512
    first = np.concatenate([np.cos(angle), -np.sin(angle)], axis=0)
    first_hi, first_lo = halves(first)
    first_in = np.concatenate([first_hi, first_hi, first_lo], axis=1)
    last_hi, last_lo = halves(first.T * 2.0**-14)
    last_out = np.concatenate([last_hi, last_hi, last_lo], axis=1)
    turn = 2 * math.pi * ((2 * freq[:, None] + 1) * coarse[None, :]) / 65536
    angle = 2 * math.pi * (coarse[:, None] * coarse[None, :] % SIDE) / SIDE
    cosine, sine = np.cos(angle), np.sin(angle)
    second = np.block([[cosine, -sine], [sine, cosine]])
    second_in = np.concatenate([halves(second)[0]] * 2 + [halves(second)[1]], axis=0)
    second_out = np.concatenate([halves(second.T)[0]] * 2 + [halves(second.T)[1]], axis=0)
    return (
        first_in,
        last_out,
        np.cos(turn).astype(np.float32),
        np.sin(turn).astype(np.float32),
        second_in,
        second_out,
    )


def split(array):
    high = array.astype(BF16)
    return high, (array - high.astype(F32)).astype(BF16)


def dot(left, right):
    return jnp.dot(left, right, preferred_element_type=F32)


def second_step(parts, table):
    high, low = split(jnp.concatenate(parts, axis=0))
    return dot(jnp.concatenate([high, low, high], axis=1), table)


def rotate(both, cosine, sine):
    turned = []
    for side in range(2):
        real = both[:SIDE, side * SIDE : (side + 1) * SIDE]
        imag = both[SIDE:, side * SIDE : (side + 1) * SIDE]
        turned.append(
            jnp.concatenate([real * cosine + imag * sine, imag * cosine - real * sine], axis=1)
        )
    return turned


def rotate_back(both, cosine, sine):
    real, imag = both[:, :SIDE], both[:, SIDE:]
    return real * cosine - imag * sine, imag * cosine + real * sine


def times(left, right):
    lr, li, rr, ri = left[:, :SIDE], left[:, SIDE:], right[:, :SIDE], right[:, SIDE:]
    return jnp.concatenate([lr * rr - li * ri, lr * ri + li * rr], axis=1)


def conj_times(left, right):
    lr, li, rr, ri = left[:, :SIDE], left[:, SIDE:], right[:, :SIDE], right[:, SIDE:]
    return jnp.concatenate([lr * rr + li * ri, lr * ri - li * rr], axis=1)


def add_conj(left, right):
    return jnp.concatenate(
        [left[:, :SIDE] + right[:, :SIDE], left[:, SIDE:] - right[:, SIDE:]], axis=1
    )


def conj(array):
    return jnp.concatenate([array[:, :SIDE], -array[:, SIDE:]], axis=1)


def kernel(
    values_hbm, gates_hbm, filters_hbm, skip_hbm, cotangent_hbm, flagged_hbm,
    first_in_hbm, last_out_hbm, cosine_hbm, sine_hbm, second_in_hbm, second_out_hbm,
    mixed, value_grad, gate_grad, ret_fg, skip_grad,
    values, gates, filters, skip, cotangent, flagged,
    first_in, last_out, cosine, sine, second_in, second_out,
    send_f, send_v, send_w, recv_f, recv_v, recv_w,
    back_mix, back_vg, back_fg, ret_mix, ret_vg,
    inner, kept_k, kept_v, kept_w, sums,
    send_sem, recv_sem, sums_send, sums_recv, fetch_sem,
):
    fetches = [
        pltpu.make_async_copy(src, dst, fetch_sem.at[i])
        for i, (src, dst) in enumerate(
            (
                (filters_hbm, filters),
                (values_hbm, values),
                (gates_hbm, gates),
                (cotangent_hbm, cotangent),
                (flagged_hbm, flagged),
                (skip_hbm, skip),
                (first_in_hbm, first_in),
                (last_out_hbm, last_out),
                (cosine_hbm, cosine),
                (sine_hbm, sine),
                (second_in_hbm, second_in),
                (second_out_hbm, second_out),
            )
        )
    ]
    fetches[0].start()

    seq = lax.axis_index("seq")
    ch = lax.axis_index("ch")
    outer = (ch == 0) | (ch == 3)
    mirror = ch // 2

    peer_ch = [jnp.where(outer, 1, 0), jnp.where(outer, 2, 3)]
    group_sign = 1 - 2 * mirror
    group_base = 127 * mirror
    mine = seq + SEQ * mirror

    x, y, rest = seq // 16, seq // 4 % 4, seq % 4
    along_x = [(x + step) % 4 * 16 for step in range(4)]
    along_y = [(y + step) % 4 * 4 for step in range(4)]

    def peers(visit):
        def some(step, carry):
            turn = (step + seq + 3 * ch) % 8
            there = [(rest + turn // 2 + k) % 4 for k in range(4)]
            even = turn % 2
            sides = [
                (even, jnp.where(even == 0, peer_ch[0], peer_ch[1])),
                (1 - even, jnp.where(even == 0, peer_ch[1], peer_ch[0])),
            ]
            for k in range(16):
                visit(along_x[k % 4] + along_y[k // 4] + there[(k + k // 4) % 4], *sides[k % 2])
            return carry

        lax.fori_loop(0, 8, some, 0)

    barrier = pltpu.get_barrier_semaphore()

    def greet(there, half, ch_there):
        pl.semaphore_signal(barrier, inc=1, device_id=(there, ch_there), device_id_type=MESH)

    circles = [
        (x, [along_x[k] + seq % 16 for k in range(1, 4)]),
        (y, [x * 16 + along_y[k] + rest for k in range(1, 4)]),
        (rest, [seq - rest + (rest + k) % 4 for k in range(1, 4)]),
    ]

    peers(greet)
    for _, others in circles:
        for there in others:
            pl.semaphore_signal(barrier, inc=1, device_id=(there, ch), device_id_type=MESH)
    for fetch in fetches[1:]:
        fetch.start()

    def remote(src, dst, which, there, ch_there):
        pltpu.make_async_remote_copy(
            src_ref=src,
            dst_ref=dst,
            send_sem=send_sem.at[which],
            recv_sem=recv_sem.at[which],
            device_id=(there, ch_there),
            device_id_type=MESH,
        ).start()

    def to_owner(src, dst, which):
        def visit(there, half, ch_there):
            group = group_base + group_sign * (half * SEQ + there)
            remote(src.at[group // 2, group % 2], dst.at[mirror * SEQ + seq], which, there, ch_there)

        peers(visit)

    def to_home(src, dst, which):
        def visit(there, half, ch_there):
            group = mine + half * (127 - 2 * mine)
            remote(src.at[half * SEQ + there], dst.at[group // 2, group % 2], which, there, ch_there)

        peers(visit)

    def wait_for(semaphores, which, ref):
        pltpu.make_async_copy(ref, ref, semaphores.at[which]).wait()

    def send_sums(stage, total):
        place, others = circles[stage]
        sums[stage, place] = total
        for there in others:
            pltpu.make_async_remote_copy(
                src_ref=sums.at[stage, place],
                dst_ref=sums.at[stage, place],
                send_sem=sums_send.at[stage],
                recv_sem=sums_recv.at[stage],
                device_id=(there, ch),
                device_id_type=MESH,
            ).start()

    def summed(stage):
        wait_for(sums_recv, stage, sums.at[stage, pl.ds(0, 3)])
        wait_for(sums_send, stage, sums.at[stage, pl.ds(0, 3)])
        return (sums[stage, 0] + sums[stage, 1]) + (sums[stage, 2] + sums[stage, 3])

    rows = lax.broadcasted_iota(jnp.int32, (16, 8, SIDE), 1) < 4

    def block(half, part):
        return pl.ds(half * SIDE, SIDE), pl.ds(part * SIDE, SIDE)

    def pack(top, bottom):
        top, bottom = top.reshape(16, 8, SIDE), bottom.reshape(16, 8, SIDE)
        even = jnp.where(rows, top, pltpu.roll(bottom, 4, 1))
        odd = jnp.where(rows, pltpu.roll(top, 4, 1), bottom)
        return even, odd

    def unpack(even, odd):
        top = jnp.where(rows, even, pltpu.roll(odd, 4, 1))
        bottom = jnp.where(rows, pltpu.roll(even, 4, 1), odd)
        return top.reshape(SIDE, SIDE), bottom.reshape(SIDE, SIDE)

    def pack_all(source, dst):
        for part in range(4):
            here = pl.ds(part * 16, 16)
            turned = [source[block(half, part)].astype(F32).T for half in range(2)]
            dst[here, 0], dst[here, 1] = pack(*turned)

    fetches[0].wait()
    pack_all(filters, send_f)
    pl.semaphore_wait(barrier, 137)
    to_owner(send_f, recv_f, 0)
    fetches[1].wait()
    pack_all(values, send_v)
    to_owner(send_v, recv_v, 1)

    for fetch in fetches[2:]:
        fetch.wait()
    flags = [
        jnp.broadcast_to(flagged[half : half + 1, :].astype(F32), (SIDE, SIDE)).T
        for half in range(2)
    ]
    totals = []
    for part in range(4):
        here = pl.ds(part * 16, 16)
        turned = []
        total = jnp.zeros((1, SIDE), F32)
        for half in range(2):
            at = block(half, part)
            product = gates[at].astype(F32) * (cotangent[at].astype(F32) * flags[half])
            inner[at] = product
            turned.append(product.T)
            total += jnp.sum(values[at].astype(F32) * product, axis=0, keepdims=True)
        send_w[here, 0], send_w[here, 1] = pack(*turned)
        totals.append(total)
    send_sums(0, jnp.concatenate(totals, axis=0))
    to_owner(send_w, recv_w, 2)

    cos_turn, sin_turn = cosine[...], sine[...]

    def load_pair(ref, pair):
        flat = ref.reshape(2 * SEQ * 8, SIDE)
        first = [flat[pl.ds(4 * half + pair, SEQ, stride=8), :] for half in range(2)]
        second = [
            flat[pl.ds(SEQ * 8 + 4 * half + 3 - pair, SEQ, stride=8), :] for half in range(2)
        ]
        return jnp.concatenate(
            [jnp.concatenate(first, axis=0), jnp.concatenate(second, axis=0)], axis=1
        )

    def store_pair(ref, pair, result):
        flat = ref.reshape(2 * SEQ * 8, SIDE)
        for half in range(2):
            top = result[half * SEQ : (half + 1) * SEQ]
            flat[pl.ds(4 * half + pair, SEQ, stride=8), :] = top[:, :SIDE]
            flat[pl.ds(SEQ * 8 + 4 * half + 3 - pair, SEQ, stride=8), :] = top[:, SIDE:]

    def first_step(signal):
        high, low = split(signal)
        return dot(first_in[...], jnp.concatenate([high, low, high], axis=0))

    def first_step_exact(signal):
        high = signal.astype(BF16)
        return dot(first_in[:, SIDE:], jnp.concatenate([high, high], axis=0))

    def spectra(stepped):
        both = second_step(rotate(stepped, cos_turn, sin_turn), second_in[...])
        return both[:SIDE], both[SIDE:]

    def inverse(first, second):
        both = second_step([first, second], second_out[...])
        r0, i0 = rotate_back(both[:SIDE], cos_turn, sin_turn)
        r1, i1 = rotate_back(both[SIDE:], cos_turn, sin_turn)
        stacked = jnp.concatenate(
            [jnp.concatenate([r0, r1], axis=1), jnp.concatenate([i0, i1], axis=1)], axis=0
        )
        high, low = split(stacked)
        return dot(last_out[...], jnp.concatenate([high, low, high], axis=0))

    wait_for(recv_sem, 0, recv_f)
    for pair in range(4):
        kept_k[pair] = add_conj(*spectra(first_step(load_pair(recv_f, pair))))
    wait_for(recv_sem, 1, recv_v)
    for pair in range(4):
        v0, v1 = spectra(first_step_exact(load_pair(recv_v, pair)))
        kept_v[pair, 0], kept_v[pair, 1] = v0, v1
        k = kept_k[pair]
        store_pair(back_mix, pair, inverse(times(k, v0), conj_times(k, v1)))
    to_home(back_mix, ret_mix, 3)
    send_sums(1, summed(0))

    wait_for(recv_sem, 2, recv_w)
    for pair in range(4):
        w0, w1 = spectra(first_step(load_pair(recv_w, pair)))
        kept_w[pair, 0], kept_w[pair, 1] = w0, w1
        k = kept_k[pair]
        store_pair(back_vg, pair, inverse(conj_times(k, w0), times(k, w1)))
    to_home(back_vg, ret_vg, 4)
    send_sums(2, summed(1))
    for pair in range(4):
        product = add_conj(
            conj_times(kept_v[pair, 0], kept_w[pair, 0]),
            conj_times(kept_v[pair, 1], kept_w[pair, 1]),
        )
        store_pair(back_fg, pair, inverse(product, conj(product)))
    to_home(back_fg, ret_fg, 5)

    def returned(ref, part):
        here = pl.ds(part * 16, 16)
        top, bottom = unpack(ref[here, 0], ref[here, 1])
        return top.T, bottom.T

    wait_for(recv_sem, 3, ret_mix)
    for part in range(4):
        for half, result in enumerate(returned(ret_mix, part)):
            at = block(half, part)
            result = result + skip[:, at[1]] * values[at].astype(F32)
            mixed[at] = (gates[at].astype(F32) * result).astype(BF16)
            gate_grad[at] = (cotangent[at].astype(F32) * flags[half] * result).astype(BF16)
    skip_grad[...] = summed(2) * 2.0**-7
    wait_for(recv_sem, 4, ret_vg)
    for part in range(4):
        for half, result in enumerate(returned(ret_vg, part)):
            at = block(half, part)
            value_grad[at] = (result + skip[:, at[1]] * inner[at]).astype(BF16)
    for which, ref in enumerate((recv_f, recv_v, recv_w, ret_mix, ret_vg, ret_fg)):
        wait_for(send_sem, which, ref)
    wait_for(recv_sem, 5, ret_fg)


def finish(*refs):
    arrived, outs, (turned, out_sem) = refs[:5], refs[5:10], refs[10:]
    stores = [
        pltpu.make_async_copy(src, dst, out_sem.at[i])
        for i, (src, dst) in enumerate(zip((*arrived[:3], turned, arrived[4]), outs))
    ]
    for i in (0, 1, 2, 4):
        stores[i].start()
    ret_fg = arrived[3]
    rows = lax.broadcasted_iota(jnp.int32, (16, 8, SIDE), 1) < 4
    for part in range(4):
        even, odd = ret_fg[pl.ds(part * 16, 16), 0], ret_fg[pl.ds(part * 16, 16), 1]
        top = jnp.where(rows, even, pltpu.roll(odd, 4, 1)).reshape(SIDE, SIDE)
        bottom = jnp.where(rows, pltpu.roll(even, 4, 1), odd).reshape(SIDE, SIDE)
        for half, result in enumerate((top, bottom)):
            turned[pl.ds(half * SIDE, SIDE), pl.ds(part * SIDE, SIDE)] = result.T * 2.0**-7
    stores[3].start()
    for store in stores:
        store.wait()


def body(values, gates, filters, skip, cotangent, flagged):
    constants = [jnp.asarray(table) for table in tables()]
    bases, width = values.shape
    hbm = pl.BlockSpec(memory_space=pltpu.HBM)
    vmem = pl.BlockSpec(memory_space=pltpu.VMEM)

    def scratch(*shape):
        return pltpu.VMEM(shape, F32)

    operands = (values, gates, filters, skip.reshape(1, width), cotangent, flagged.reshape(2, SIDE))
    halfwords = jax.ShapeDtypeStruct((bases, width), BF16)
    home = (GROUPS // 2, 2, 8, SIDE)
    owner = (GROUPS, 8, SIDE)
    outs = pl.pallas_call(
        kernel,
        out_shape=[
            halfwords,
            halfwords,
            halfwords,
            jax.ShapeDtypeStruct(home, F32),
            jax.ShapeDtypeStruct((4, SIDE), F32),
        ],
        in_specs=[hbm] * 12,
        out_specs=[vmem] * 5,
        scratch_shapes=[
            *[pltpu.VMEM(array.shape, array.dtype) for array in (*operands, *constants)],
            *[scratch(*home)] * 3,
            *[scratch(*owner)] * 6,
            *[scratch(*home)] * 2,
            scratch(bases, width),
            scratch(4, SIDE, 2 * SIDE),
            *[scratch(4, 2, SIDE, 2 * SIDE)] * 2,
            scratch(3, 4, 4, SIDE),
            pltpu.SemaphoreType.DMA((6,)),
            pltpu.SemaphoreType.DMA((6,)),
            pltpu.SemaphoreType.DMA((3,)),
            pltpu.SemaphoreType.DMA((3,)),
            pltpu.SemaphoreType.DMA((12,)),
        ],
        compiler_params=pltpu.CompilerParams(
            collective_id=0, has_side_effects=True, vmem_limit_bytes=28 << 20
        ),
        name="hyena",
    )(*[pltpu.with_memory_space_constraint(array, pltpu.HBM) for array in (*operands, *constants)])
    outs = pl.pallas_call(
        finish,
        out_shape=[
            halfwords,
            halfwords,
            halfwords,
            jax.ShapeDtypeStruct((bases, width), F32),
            jax.ShapeDtypeStruct((4, SIDE), F32),
        ],
        in_specs=[vmem] * 5,
        out_specs=[hbm] * 5,
        scratch_shapes=[scratch(bases, width), pltpu.SemaphoreType.DMA((5,))],
        compiler_params=pltpu.CompilerParams(vmem_limit_bytes=28 << 20),
        name="finish",
    )(*outs)
    return (*outs[:4], outs[4].reshape(width))


def solution(mesh):
    placed = (P("seq", "ch"), P("seq", "ch"), P("seq", "ch"), P("ch"), P("seq", "ch"), P("seq"))
    return jax.shard_map(
        body,
        mesh=mesh,
        in_specs=placed,
        out_specs=(P("seq", "ch"), P("seq", "ch"), P("seq", "ch"), P("seq", "ch"), P("ch")),
        check_vma=False,
    )
```

time: 101 us -> 87.1 us (0.86)
  local copies, waits for them, and re-layouts: 13.6 us -> 0 us
    unnamed x29 -> x0, local copies, waits for them, and re-layouts: 13.6 us -> none
    pallas_call x1 -> x2, Pallas kernels: 86.3 us -> 86.4 us  [the longest x1 85.3 us: body(): pl.pallas_call(kernel, out_shape=[halfwords, halfwords, halfwords, jax.Sh...]
where the time goes in v2:
time: 87.1 us
  Pallas kernels  86.4 us (99%)
    pallas_call x1, Pallas kernels, body(): pl.pallas_call(kernel, out_shape=[halfwords, halfwords, halfwords, jax.Sh...  85.3 us

profile of v2, /device:TPU:1, one launch (start us, length us, event | category | flops | bytes accessed | tf_op | source)
XLA Modules:
  0.0 87.1 jit_solution(6751309366425165781)
XLA Ops:
  0.6 85.3 %hyena.1 = (bf16[256,512]{1,0:T(8,128)(2,1)S(1)}, bf16[256,512]{1,0:T(8,128)(2,1)S(1)}, bf16[256,512]{1,0:T(8,128)(2,1)S(1)}, f32[64,2,8,128]{3,2,1,0:T(8,128)S(1)}, f32[4,128]{1,0:T(4,128)S(1)}) custom-call(bf16[256,512]{1,0:T(8,128)(2,1)} %values_hbm.1, bf16[256,512]{1,0:T(8,128)(2,1)} %gates_hbm.1, f32[256,512]{1,0:T(8,128)} %filters_hbm.1, ...), custom_call_target="tpu_custom_call" | custom-call | tf_op jit(solution)/shard_map/hyena/pallas_call | solution.py:405
  86.0 1.1 %finish.1 = (bf16[256,512]{1,0:T(8,128)(2,1)}, bf16[256,512]{1,0:T(8,128)(2,1)}, bf16[256,512]{1,0:T(8,128)(2,1)}, f32[256,512]{1,0:T(8,128)}, f32[4,128]{1,0:T(4,128)}) custom-call(bf16[256,512]{1,0:T(8,128)(2,1)S(1)} %get-tuple-element.15.refs_0_, bf16[256,512]{1,0:T(8,128)(2,1)S(1)} %get-tuple-element.16.refs_1_, ...), custom_call_target="tpu_custom_call" | custom-call | tf_op jit(solution)/shard_map/finish/pallas_call | solution.py:436

commit v3 on v2

--- a/solution.py
+++ b/solution.py
@@ -106,7 +106,7 @@
     mixed, value_grad, gate_grad, ret_fg, skip_grad,
     values, gates, filters, skip, cotangent, flagged,
     first_in, last_out, cosine, sine, second_in, second_out,
-    send_f, send_v, send_w, recv_f, recv_v, recv_w,
+    send_fv, send_w, recv_fv, recv_w,
     back_mix, back_vg, back_fg, ret_mix, ret_vg,
     inner, kept_k, kept_v, kept_w, sums,
     send_sem, recv_sem, sums_send, sums_recv, fetch_sem,
@@ -146,20 +146,17 @@
     along_x = [(x + step) % 4 * 16 for step in range(4)]
     along_y = [(y + step) % 4 * 4 for step in range(4)]
 
+    along_rest = [(rest + step) % 4 for step in range(4)]
+
     def peers(visit):
         def some(step, carry):
-            turn = (step + seq + 3 * ch) % 8
-            there = [(rest + turn // 2 + k) % 4 for k in range(4)]
-            even = turn % 2
-            sides = [
-                (even, jnp.where(even == 0, peer_ch[0], peer_ch[1])),
-                (1 - even, jnp.where(even == 0, peer_ch[1], peer_ch[0])),
-            ]
-            for k in range(16):
-                visit(along_x[k % 4] + along_y[k // 4] + there[(k + k // 4) % 4], *sides[k % 2])
+            far_x = (x + jnp.where(step == 0, 2, jnp.where(step == 3, 0, 2 * step - 1))) % 4 * 16
+            for far_y in (2, 1, 3, 0):
+                for k in range(8):
+                    visit(far_x + along_y[far_y] + along_rest[k % 4], k // 4, peer_ch[k // 4])
             return carry
 
-        lax.fori_loop(0, 8, some, 0)
+        lax.fori_loop(0, 4, some, 0)
 
     barrier = pltpu.get_barrier_semaphore()
 
@@ -240,19 +237,18 @@
         bottom = jnp.where(rows, pltpu.roll(even, 4, 1), odd)
         return top.reshape(SIDE, SIDE), bottom.reshape(SIDE, SIDE)
 
-    def pack_all(source, dst):
+    def pack_all(source, dst, which):
         for part in range(4):
             here = pl.ds(part * 16, 16)
             turned = [source[block(half, part)].astype(F32).T for half in range(2)]
-            dst[here, 0], dst[here, 1] = pack(*turned)
+            dst[here, 0, which], dst[here, 1, which] = pack(*turned)
 
     fetches[0].wait()
-    pack_all(filters, send_f)
+    pack_all(filters, send_fv, 0)
+    fetches[1].wait()
+    pack_all(values, send_fv, 1)
     pl.semaphore_wait(barrier, 137)
-    to_owner(send_f, recv_f, 0)
-    fetches[1].wait()
-    pack_all(values, send_v)
-    to_owner(send_v, recv_v, 1)
+    to_owner(send_fv, recv_fv, 0)
 
     for fetch in fetches[2:]:
         fetch.wait()
@@ -278,12 +274,14 @@
 
     cos_turn, sin_turn = cosine[...], sine[...]
 
-    def load_pair(ref, pair):
-        flat = ref.reshape(2 * SEQ * 8, SIDE)
-        first = [flat[pl.ds(4 * half + pair, SEQ, stride=8), :] for half in range(2)]
-        second = [
-            flat[pl.ds(SEQ * 8 + 4 * half + 3 - pair, SEQ, stride=8), :] for half in range(2)
+    def load_pair(ref, pair, which=0, count=1):
+        flat = ref.reshape(2 * SEQ * count * 8, SIDE)
+        stride = count * 8
+        first = [
+            flat[pl.ds(which * 8 + 4 * half + pair, SEQ, stride=stride), :] for half in range(2)
         ]
+        start = SEQ * stride + which * 8 + 3 - pair
+        second = [flat[pl.ds(start + 4 * half, SEQ, stride=stride), :] for half in range(2)]
         return jnp.concatenate(
             [jnp.concatenate(first, axis=0), jnp.concatenate(second, axis=0)], axis=1
         )
@@ -317,12 +315,11 @@
         high, low = split(stacked)
         return dot(last_out[...], jnp.concatenate([high, low, high], axis=0))
 
-    wait_for(recv_sem, 0, recv_f)
+    wait_for(recv_sem, 0, recv_fv)
     for pair in range(4):
-        kept_k[pair] = add_conj(*spectra(first_step(load_pair(recv_f, pair))))
-    wait_for(recv_sem, 1, recv_v)
+        kept_k[pair] = add_conj(*spectra(first_step(load_pair(recv_fv, pair, 0, 2))))
     for pair in range(4):
-        v0, v1 = spectra(first_step_exact(load_pair(recv_v, pair)))
+        v0, v1 = spectra(first_step_exact(load_pair(recv_fv, pair, 1, 2)))
         kept_v[pair, 0], kept_v[pair, 1] = v0, v1
         k = kept_k[pair]
         store_pair(back_mix, pair, inverse(times(k, v0), conj_times(k, v1)))
@@ -363,7 +360,7 @@
         for half, result in enumerate(returned(ret_vg, part)):
             at = block(half, part)
             value_grad[at] = (result + skip[:, at[1]] * inner[at]).astype(BF16)
-    for which, ref in enumerate((recv_f, recv_v, recv_w, ret_mix, ret_vg, ret_fg)):
+    for which, ref in ((0, recv_fv), (2, recv_w), (3, ret_mix), (4, ret_vg), (5, ret_fg)):
         wait_for(send_sem, which, ref)
     wait_for(recv_sem, 5, ret_fg)
 
@@ -415,8 +412,10 @@
         out_specs=[vmem] * 5,
         scratch_shapes=[
             *[pltpu.VMEM(array.shape, array.dtype) for array in (*operands, *constants)],
-            *[scratch(*home)] * 3,
-            *[scratch(*owner)] * 6,
+            scratch(GROUPS // 2, 2, 2, 8, SIDE),
+            scratch(*home),
+            scratch(GROUPS, 2, 8, SIDE),
+            *[scratch(*owner)] * 4,
             *[scratch(*home)] * 2,
             scratch(bases, width),
             scratch(4, SIDE, 2 * SIDE),

time: 87.1 us -> 84.8 us (0.974)
  Pallas kernels: 86.4 us -> 84.1 us
    pallas_call x1, Pallas kernels: 85.3 us -> 83 us  [body(): pl.pallas_call(kernel, out_shape=[halfwords, halfwords, halfwords, jax.Sh...]
where the time goes in v3:
time: 84.8 us; the launch traced here: 84.7 us
  Pallas kernels  84.1 us (99%)
    pallas_call x1, Pallas kernels, body(): pl.pallas_call(kernel, out_shape=[halfwords, halfwords, halfwords, jax.Sh...  83 us

profile of v3, /device:TPU:1, one launch (start us, length us, event | category | flops | bytes accessed | tf_op | source)
XLA Modules:
  0.0 84.7 jit_solution(13799926832239692597)
XLA Ops:
  0.6 83.0 %hyena.1 = (bf16[256,512]{1,0:T(8,128)(2,1)S(1)}, bf16[256,512]{1,0:T(8,128)(2,1)S(1)}, bf16[256,512]{1,0:T(8,128)(2,1)S(1)}, f32[64,2,8,128]{3,2,1,0:T(8,128)S(1)}, f32[4,128]{1,0:T(4,128)S(1)}) custom-call(bf16[256,512]{1,0:T(8,128)(2,1)} %values_hbm.1, bf16[256,512]{1,0:T(8,128)(2,1)} %gates_hbm.1, f32[256,512]{1,0:T(8,128)} %filters_hbm.1, ...), custom_call_target="tpu_custom_call" | custom-call | tf_op jit(solution)/shard_map/hyena/pallas_call | solution.py:402
  83.6 1.1 %finish.1 = (bf16[256,512]{1,0:T(8,128)(2,1)}, bf16[256,512]{1,0:T(8,128)(2,1)}, bf16[256,512]{1,0:T(8,128)(2,1)}, f32[256,512]{1,0:T(8,128)}, f32[4,128]{1,0:T(4,128)}) custom-call(bf16[256,512]{1,0:T(8,128)(2,1)S(1)} %get-tuple-element.15.refs_0_, bf16[256,512]{1,0:T(8,128)(2,1)S(1)} %get-tuple-element.16.refs_1_, ...), custom_call_target="tpu_custom_call" | custom-call | tf_op jit(solution)/shard_map/finish/pallas_call | solution.py:435

commit v4 on v3

--- a/solution.py
+++ b/solution.py
@@ -109,7 +109,7 @@
     send_fv, send_w, recv_fv, recv_w,
     back_mix, back_vg, back_fg, ret_mix, ret_vg,
     inner, kept_k, kept_v, kept_w, sums,
-    send_sem, recv_sem, sums_send, sums_recv, fetch_sem,
+    send_sem, recv_sem, sums_send, sums_recv, fetch_sem, ready,
 ):
     fetches = [
         pltpu.make_async_copy(src, dst, fetch_sem.at[i])
@@ -148,15 +148,22 @@
 
     along_rest = [(rest + step) % 4 for step in range(4)]
 
-    def peers(visit):
+    def column(there, visit):
+        for k in range(8):
+            visit(there + along_rest[k % 4], k // 4, peer_ch[k // 4])
+
+    def peers(visit, near=True):
         def some(step, carry):
-            far_x = (x + jnp.where(step == 0, 2, jnp.where(step == 3, 0, 2 * step - 1))) % 4 * 16
+            far_x = (x + jnp.where(step == 0, 2, 2 * step - 1)) % 4 * 16
             for far_y in (2, 1, 3, 0):
-                for k in range(8):
-                    visit(far_x + along_y[far_y] + along_rest[k % 4], k // 4, peer_ch[k // 4])
+                column(far_x + along_y[far_y], visit)
             return carry
 
-        lax.fori_loop(0, 4, some, 0)
+        lax.fori_loop(0, 3, some, 0)
+        for far_y in (2, 1, 3):
+            column(x * 16 + along_y[far_y], visit)
+        if near:
+            column(seq - rest, visit)
 
     barrier = pltpu.get_barrier_semaphore()
 
@@ -169,10 +176,10 @@
         (rest, [seq - rest + (rest + k) % 4 for k in range(1, 4)]),
     ]
 
-    peers(greet)
-    for _, others in circles:
-        for there in others:
-            pl.semaphore_signal(barrier, inc=1, device_id=(there, ch), device_id_type=MESH)
+    column(seq - rest, greet)
+    plane = [px + py + rest for px in along_x for py in along_y][1:]
+    for there in (*circles[2][1], *plane):
+        pl.semaphore_signal(barrier, inc=1, device_id=(there, ch), device_id_type=MESH)
     for fetch in fetches[1:]:
         fetch.start()
 
@@ -191,7 +198,7 @@
             group = group_base + group_sign * (half * SEQ + there)
             remote(src.at[group // 2, group % 2], dst.at[mirror * SEQ + seq], which, there, ch_there)
 
-        peers(visit)
+        return visit
 
     def to_home(src, dst, which):
         def visit(there, half, ch_there):
@@ -247,8 +254,12 @@
     pack_all(filters, send_fv, 0)
     fetches[1].wait()
     pack_all(values, send_fv, 1)
-    pl.semaphore_wait(barrier, 137)
-    to_owner(send_fv, recv_fv, 0)
+    pl.semaphore_wait(barrier, 26)
+    for there in plane:
+        pl.semaphore_signal(ready, inc=1, device_id=(there, ch), device_id_type=MESH)
+    column(seq - rest, to_owner(send_fv, recv_fv, 0))
+    pl.semaphore_wait(ready, 15)
+    peers(to_owner(send_fv, recv_fv, 0), near=False)
 
     for fetch in fetches[2:]:
         fetch.wait()
@@ -270,7 +281,7 @@
         send_w[here, 0], send_w[here, 1] = pack(*turned)
         totals.append(total)
     send_sums(0, jnp.concatenate(totals, axis=0))
-    to_owner(send_w, recv_w, 2)
+    peers(to_owner(send_w, recv_w, 2))
 
     cos_turn, sin_turn = cosine[...], sine[...]
 
@@ -426,6 +437,7 @@
             pltpu.SemaphoreType.DMA((3,)),
             pltpu.SemaphoreType.DMA((3,)),
             pltpu.SemaphoreType.DMA((12,)),
+            pltpu.SemaphoreType.REGULAR,
         ],
         compiler_params=pltpu.CompilerParams(
             collective_id=0, has_side_effects=True, vmem_limit_bytes=28 << 20

time: 84.8 us -> 84.4 us (level)
  no operation moved by 1% of the time
where the time goes in v4:
time: 84.4 us; the launch traced here: 84.3 us
  Pallas kernels  83.7 us (99%)
    pallas_call x1, Pallas kernels, body(): pl.pallas_call(kernel, out_shape=[halfwords, halfwords, halfwords, jax.Sh...  82.6 us

profile of v4, /device:TPU:1, one launch (start us, length us, event | category | flops | bytes accessed | tf_op | source)
XLA Modules:
  0.0 84.3 jit_solution(14301048636266814287)
XLA Ops:
  0.6 82.6 %hyena.1 = (bf16[256,512]{1,0:T(8,128)(2,1)S(1)}, bf16[256,512]{1,0:T(8,128)(2,1)S(1)}, bf16[256,512]{1,0:T(8,128)(2,1)S(1)}, f32[64,2,8,128]{3,2,1,0:T(8,128)S(1)}, f32[4,128]{1,0:T(4,128)S(1)}) custom-call(bf16[256,512]{1,0:T(8,128)(2,1)} %values_hbm.1, bf16[256,512]{1,0:T(8,128)(2,1)} %gates_hbm.1, f32[256,512]{1,0:T(8,128)} %filters_hbm.1, ...), custom_call_target="tpu_custom_call" | custom-call | tf_op jit(solution)/shard_map/hyena/pallas_call | solution.py:413
  83.2 1.1 %finish.1 = (bf16[256,512]{1,0:T(8,128)(2,1)}, bf16[256,512]{1,0:T(8,128)(2,1)}, bf16[256,512]{1,0:T(8,128)(2,1)}, f32[256,512]{1,0:T(8,128)}, f32[4,128]{1,0:T(4,128)}) custom-call(bf16[256,512]{1,0:T(8,128)(2,1)S(1)} %get-tuple-element.15.refs_0_, bf16[256,512]{1,0:T(8,128)(2,1)S(1)} %get-tuple-element.16.refs_1_, ...), custom_call_target="tpu_custom_call" | custom-call | tf_op jit(solution)/shard_map/finish/pallas_call | solution.py:447
